TPU v7x, 512 devices: a whole 4x4x16 slice. The times are simulated.
512 devices in a mesh: rows: 64 (over y_hi, z, core), cols: 8 (over x, y_lo).
Axes of the slice: x: 4, y: 4 (y_hi: 2, y_lo: 2; y = y_hi * 2 + y_lo), z: 16, core: 2. Of those that a mesh axis runs over, the one named last changes fastest.
Arguments:
- low_frames: bfloat16 [256, 128, 128], P('rows', 'cols'), may hold values from -6 to 6
- conv_weight: bfloat16 [3456, 128], replicated, may hold values from -0.109375 to 0.109375
- attn_in: bfloat16 [128, 384], replicated, may hold values from -2 to 2
- attn_out: bfloat16 [128, 128], replicated, may hold values from -0.5 to 0.5
Outputs:
- refined: bfloat16 [1024, 512, 128], P('rows', 'cols')
All inputs are finite; a program needn't handle non-finite values.
Results may differ from a plain program's by a relative error of at most 0.0068.
Values may be sent and summed in bfloat16 or wider, within the bound.
A program may use at most 64 MiB of HBM per device.

v0:
```python
import jax
import jax.numpy as jnp
from jax import lax
from jax.sharding import PartitionSpec as P

HEADS = 2
BANDS = 2


def from_behind(block, axis, distance):
    devices = range(lax.axis_size(axis))
    route = [(i - distance, i) for i in devices if i - distance in devices]
    return lax.ppermute(block, axis, route)


def padded(block, sides, width):
    for axis, dim in sides:
        count = lax.axis_size(axis)
        forward = [(i, i + 1) for i in range(count - 1)]
        backward = [(target, source) for source, target in forward]
        low = lax.ppermute(
            lax.slice_in_dim(block, block.shape[dim] - width, None, axis=dim), axis, forward
        )
        high = lax.ppermute(lax.slice_in_dim(block, 0, width, axis=dim), axis, backward)
        block = jnp.concatenate([low, block, high], axis=dim)
    return block


def upsample_axis(values, axis):
    count = values.shape[axis] - 2

    def sliced(begin, end):
        return lax.slice_in_dim(values, begin, end, axis=axis)

    before = sliced(0, count)
    centre = sliced(1, count + 1)
    behind = sliced(2, count + 2)
    phases = jnp.stack(
        [
            0.375 * before + 0.625 * centre,
            0.125 * before + 0.875 * centre,
            0.875 * centre + 0.125 * behind,
            0.625 * centre + 0.375 * behind,
        ],
        axis=axis + 1,
    )
    target = list(centre.shape)
    target[axis] = 4 * count
    middle = phases.reshape(target)
    opening = 0.625 * sliced(0, 1) + 0.375 * sliced(1, 2)
    closing = 0.375 * sliced(count, count + 1) + 0.625 * sliced(count + 1, count + 2)
    return jnp.concatenate([opening, middle, closing], axis=axis)


def lift_block(block, top_edge, bottom_edge, left_edge, right_edge):
    higher = upsample_axis(upsample_axis(block.astype(jnp.float32), 0), 1).astype(jnp.bfloat16)
    row_ids = lax.broadcasted_iota(jnp.int32, higher.shape, 0)
    col_ids = lax.broadcasted_iota(jnp.int32, higher.shape, 1)
    outside = (row_ids == 0) & top_edge | (row_ids == higher.shape[0] - 1) & bottom_edge
    outside = outside | (col_ids == 0) & left_edge | (col_ids == higher.shape[1] - 1) & right_edge
    return jnp.where(outside, jnp.zeros_like(higher), higher)


def band_edge(piece, offset):
    return from_behind(piece, "rows", offset)


def shift_high(block, offset):
    return from_behind(block, "rows", offset)


def attend_projected(projected):
    groups = projected.shape[0]
    items = projected.shape[2]
    chans = projected.shape[3] // 3
    head_size = chans // HEADS
    frames = groups // BANDS
    shaped = projected.reshape(BANDS, frames, items, 3, HEADS, head_size)
    scores = jnp.einsum(
        "bfmhd,bgmhd->bmhfg",
        shaped[:, :, :, 0],
        shaped[:, :, :, 1],
        preferred_element_type=jnp.float32,
    ) / jnp.sqrt(jnp.float32(head_size))
    scores = scores - jnp.max(scores, axis=-1, keepdims=True)
    expo = jnp.exp(scores)
    weights = (expo / jnp.sum(expo, axis=-1, keepdims=True)).astype(jnp.bfloat16)
    context = jnp.einsum(
        "bmhfg,bgmhd->bfmhd", weights, shaped[:, :, :, 2], preferred_element_type=jnp.float32
    ).astype(jnp.bfloat16)
    context = context.reshape(groups, 1, items, chans)
    return lax.all_to_all(context, "rows", split_axis=0, concat_axis=1, tiled=True)


def local(low_frames, conv_weight, attn_in, attn_out):
    rows_low, cols_low, chans = low_frames.shape
    groups = lax.axis_size("rows")
    frames = groups // BANDS
    place = lax.axis_index("rows")
    band = place // frames
    frame = place % frames
    column = lax.axis_index("cols")
    last_column = lax.axis_size("cols") - 1
    wide = padded(low_frames, (("cols", 1),), 1)
    col_ids = lax.broadcasted_iota(jnp.int32, wide.shape, 1)
    wide = jnp.where((col_ids == 0) & (column == 0), wide[:, 1:2], wide)
    wide = jnp.where(
        (col_ids == cols_low + 1) & (column == last_column), wide[:, cols_low : cols_low + 1], wide
    )
    above = band_edge(wide[rows_low - 1 : rows_low], frames)
    below = band_edge(wide[0:1], -frames)
    above = jnp.where(band == 0, wide[0:1], above)
    below = jnp.where(band == BANDS - 1, wide[rows_low - 1 : rows_low], below)
    extended = jnp.concatenate([above, wide, below], axis=0)
    top_edge = band == 0
    bottom_edge = band == BANDS - 1
    left_edge = column == 0
    right_edge = column == last_column
    current = lift_block(extended, top_edge, bottom_edge, left_edge, right_edge)
    earlier = shift_high(current, 1)
    later = shift_high(current, -1)
    earlier = jnp.where(frame == 0, jnp.zeros_like(earlier), earlier)
    later = jnp.where(frame == frames - 1, jnp.zeros_like(later), later)
    rows_high = 4 * rows_low
    cols_high = 4 * cols_low
    pixels = rows_high * cols_high
    taps = conv_weight.reshape(9, 3 * chans, chans)
    slabs = (earlier, current, later)
    total = jnp.zeros((pixels, chans), jnp.float32)
    for tap_t in range(3):
        for tap_y in range(3):
            window = jnp.concatenate(
                [
                    slabs[tap_t][tap_y : tap_y + rows_high, offset : offset + cols_high]
                    for offset in range(3)
                ],
                axis=-1,
            ).reshape(pixels, 3 * chans)
            total = total + jnp.dot(
                window, taps[3 * tap_t + tap_y], preferred_element_type=jnp.float32
            )
    features = (
        current[1:-1, 1:-1].reshape(pixels, chans).astype(jnp.float32) + jax.nn.silu(total)
    ).astype(jnp.bfloat16)
    per_group = pixels // groups
    projected = jnp.dot(features, attn_in, preferred_element_type=jnp.float32).astype(jnp.bfloat16)
    context = attend_projected(
        lax.all_to_all(
            projected.reshape(1, groups, per_group, 3 * chans),
            "rows",
            split_axis=1,
            concat_axis=0,
            tiled=True,
        )
    )
    output = jnp.dot(context.reshape(pixels, chans), attn_out, preferred_element_type=jnp.float32)
    refined = (features.astype(jnp.float32) + output).astype(jnp.bfloat16)
    return refined.reshape(rows_high, cols_high, chans)


def solution(mesh):
    in_specs = (P("rows", "cols", None), P(), P(), P())
    out_specs = P("rows", "cols", None)
    return jax.shard_map(local, mesh=mesh, in_specs=in_specs, out_specs=out_specs, check_vma=False)
```

profile of v0, /device:TPU:1, one launch (start us, length us, event | category | flops | bytes accessed | tf_op | source)
XLA Modules:
  0.0 136.0 jit_solution(9024993678474585741)
XLA Ops:
  0.0 0.8 copy.18
  0.8 1.3 collective-permute-start.1
  2.1 4.7 %collective-permute-start = (bf16[4,1,128]{2,0,1:T(4,128)(2,1)S(1)}, bf16[4,1,128]{2,0,1:T(4,128)(2,1)S(1)}, u32[]{:S(2)}, u32[]{:S(2)}) collective-permute-start(bf16[4,1,128]{2,0,1:T(4,128)(2,1)S(1)} %get-tuple-element.52), channel_id=1, source_target_pairs={{0,1},{1,2},{2,3},{3,4},{4,5},{5,6},{6,7},{8,9},{9,10},{10,11},{11... | collective-permute-start | bytes 3080 | tf_op jit(solution)/shard_map/ppermute | solution.py:21
  6.8 0.6 collective-permute-done
  7.7 5.0 %collective-permute-start.2 = (bf16[1,18,128]{2,0,1:T(2,128)(2,1)S(1)}, bf16[1,18,128]{2,0,1:T(2,128)(2,1)S(1)}, u32[]{:S(2)}, u32[]{:S(2)}) collective-permute-start(bf16[1,18,128]{2,0,1:T(2,128)(2,1)S(1)} %get-tuple-element.49), channel_id=1, source_target_pairs={{0,256},{8,264},{16,272},{24,280},{32,288},{40,296},{48,304},{56,3... | collective-permute-start | bytes 13832 | tf_op jit(solution)/shard_map/ppermute | solution.py:13
  12.7 1.3 collective-permute-start.3
  14.0 4.6 %collective-permute-done.3 = bf16[1,18,128]{2,0,1:T(2,128)(2,1)S(1)} collective-permute-done((bf16[1,18,128]{2,0,1:T(2,128)(2,1)S(1)}, bf16[1,18,128]{2,0,1:T(2,128)(2,1)S(1)}, u32[]{:S(2)}, u32[]{:S(2)}) %collective-permute-start.3) | collective-permute-done | bytes 4640 | tf_op jit(solution)/shard_map/ppermute | solution.py:13
  19.5 0.4 or_select_fusion
  19.8 0.5 fusion.31
  20.3 6.7 %collective-permute-start.4 = (bf16[18,66,128]{2,1,0:T(8,128)(2,1)S(1)}, bf16[18,66,128]{2,1,0:T(8,128)(2,1)S(1)}, u32[]{:S(2)}, u32[]{:S(2)}) collective-permute-start(bf16[18,66,128]{2,1,0:T(8,128)(2,1)S(1)} %or_select_fusion), channel_id=1, source_target_pairs={{0,8},{8,16},{16,24},{24,32},{32,40},{40,48},{48,56},{56,64},{64,7... | collective-permute-start | bytes 912392 | tf_op jit(solution)/shard_map/ppermute | solution.py:13
  27.0 1.9 %collective-permute-start.5 = (bf16[18,66,128]{2,1,0:T(8,128)(2,1)S(1)}, bf16[18,66,128]{2,1,0:T(8,128)(2,1)S(1)}, u32[]{:S(2)}, u32[]{:S(2)}) collective-permute-start(bf16[18,66,128]{2,1,0:T(8,128)(2,1)S(1)} %or_select_fusion), channel_id=1, source_target_pairs={{8,0},{16,8},{24,16},{32,24},{40,32},{48,40},{56,48},{64,56},{72,6... | collective-permute-start | bytes 912392 | tf_op jit(solution)/shard_map/ppermute | solution.py:13
  29.3 1.8 %collective-permute-done.4 = bf16[18,66,128]{2,1,0:T(8,128)(2,1)S(1)} collective-permute-done((bf16[18,66,128]{2,1,0:T(8,128)(2,1)S(1)}, bf16[18,66,128]{2,1,0:T(8,128)(2,1)S(1)}, u32[]{:S(2)}, u32[]{:S(2)}) %collective-permute-start.4) | collective-permute-done | bytes 304160 | tf_op jit(solution)/shard_map/ppermute | solution.py:13
  31.1 0.5 fusion.32
  31.5 3.9 %collective-permute-done.5 = bf16[18,66,128]{2,1,0:T(8,128)(2,1)S(1)} collective-permute-done((bf16[18,66,128]{2,1,0:T(8,128)(2,1)S(1)}, bf16[18,66,128]{2,1,0:T(8,128)(2,1)S(1)}, u32[]{:S(2)}, u32[]{:S(2)}) %collective-permute-start.5) | collective-permute-done | bytes 304160 | tf_op jit(solution)/shard_map/ppermute | solution.py:13
  35.5 0.5 fusion.30
  36.1 1.0 copy-done.1
  37.6 0.4 convolution_add_fusion.8
  38.1 0.4 convolution_add_fusion.7
  38.5 0.4 convolution_add_fusion.6
  38.8 0.4 convolution_add_fusion.5
  39.2 0.4 convolution_add_fusion.4
  40.2 0.4 convolution_add_fusion.2
  40.7 0.4 fusion.5
  41.5 57.4 %all_to_all.8 = bf16[1,64,16,384]{3,2,0,1:T(8,128)(2,1)S(1)} all-to-all(bf16[1,64,16,384]{3,2,0,1:T(8,128)(2,1)S(1)} %bitcast.76), channel_id=1, replica_groups=mesh['rows'=64,'cols'=8] {'rows'}, dimensions={1} | all-to-all | bytes 1572864 | tf_op jit(solution)/shard_map/all_to_all | solution.py:148
  98.9 0.8 reshape.93
  99.7 1.2 fusion.29
  100.9 0.7 fusion.34
  101.6 0.5 convolution_multiply_fusion
  102.0 0.5 fusion.3
  102.6 0.4 copy.30
  103.3 31.8 %all_to_all.9 = bf16[64,1,16,128]{3,2,1,0:T(8,128)(2,1)S(1)} all-to-all(bf16[64,1,16,128]{3,2,1,0:T(8,128)(2,1)S(1)} %bitcast.89), channel_id=1, replica_groups=mesh['rows'=64,'cols'=8] {'rows'}, dimensions={0} | all-to-all | bytes 524288 | tf_op jit(solution)/shard_map/all_to_all | solution.py:92
  135.1 0.9 fusion.4
  (44 shorter events, 3.4 us)
Async XLA Ops:
  0.0 41.1 %copy-start = (bf16[128,384]{1,0:T(8,128)(2,1)S(1)}, bf16[128,384]{1,0:T(8,128)(2,1)}, u32[]{:S(2)}) copy-start(bf16[128,384]{1,0:T(8,128)(2,1)} %param.6) | copy-start | bytes 294916
  0.8 6.0 %collective-permute-start.1 = (bf16[4,1,128]{2,0,1:T(4,128)(2,1)S(1)}, bf16[4,1,128]{2,0,1:T(4,128)(2,1)S(1)}, u32[]{:S(2)}, u32[]{:S(2)}) collective-permute-start(bf16[4,1,128]{2,0,1:T(4,128)(2,1)S(1)} %get-tuple-element.53), channel_id=1, source_target_pairs={{1,0},{2,1},{3,2},{4,3},{5,4},{6,5},{7,6},{9,8},{10,9},{11,10},{12... | collective-permute-start | bytes 3080 | tf_op jit(solution)/shard_map/ppermute | solution.py:24
  2.1 5.4 %collective-permute-start = (bf16[4,1,128]{2,0,1:T(4,128)(2,1)S(1)}, bf16[4,1,128]{2,0,1:T(4,128)(2,1)S(1)}, u32[]{:S(2)}, u32[]{:S(2)}) collective-permute-start(bf16[4,1,128]{2,0,1:T(4,128)(2,1)S(1)} %get-tuple-element.52), channel_id=1, source_target_pairs={{0,1},{1,2},{2,3},{3,4},{4,5},{5,6},{6,7},{8,9},{9,10},{10,11},{11... | collective-permute-start | bytes 3080 | tf_op jit(solution)/shard_map/ppermute | solution.py:21
  7.7 6.3 %collective-permute-start.2 = (bf16[1,18,128]{2,0,1:T(2,128)(2,1)S(1)}, bf16[1,18,128]{2,0,1:T(2,128)(2,1)S(1)}, u32[]{:S(2)}, u32[]{:S(2)}) collective-permute-start(bf16[1,18,128]{2,0,1:T(2,128)(2,1)S(1)} %get-tuple-element.49), channel_id=1, source_target_pairs={{0,256},{8,264},{16,272},{24,280},{32,288},{40,296},{48,304},{56,3... | collective-permute-start | bytes 13832 | tf_op jit(solution)/shard_map/ppermute | solution.py:13
  12.7 5.9 %collective-permute-start.3 = (bf16[1,18,128]{2,0,1:T(2,128)(2,1)S(1)}, bf16[1,18,128]{2,0,1:T(2,128)(2,1)S(1)}, u32[]{:S(2)}, u32[]{:S(2)}) collective-permute-start(bf16[1,18,128]{2,0,1:T(2,128)(2,1)S(1)} %get-tuple-element.50), channel_id=1, source_target_pairs={{256,0},{264,8},{272,16},{280,24},{288,32},{296,40},{304,48},{312,... | collective-permute-start | bytes 13832 | tf_op jit(solution)/shard_map/ppermute | solution.py:13
  20.3 10.7 %collective-permute-start.4 = (bf16[18,66,128]{2,1,0:T(8,128)(2,1)S(1)}, bf16[18,66,128]{2,1,0:T(8,128)(2,1)S(1)}, u32[]{:S(2)}, u32[]{:S(2)}) collective-permute-start(bf16[18,66,128]{2,1,0:T(8,128)(2,1)S(1)} %or_select_fusion), channel_id=1, source_target_pairs={{0,8},{8,16},{16,24},{24,32},{32,40},{40,48},{48,56},{56,64},{64,7... | collective-permute-start | bytes 912392 | tf_op jit(solution)/shard_map/ppermute | solution.py:13
  27.0 8.4 %collective-permute-start.5 = (bf16[18,66,128]{2,1,0:T(8,128)(2,1)S(1)}, bf16[18,66,128]{2,1,0:T(8,128)(2,1)S(1)}, u32[]{:S(2)}, u32[]{:S(2)}) collective-permute-start(bf16[18,66,128]{2,1,0:T(8,128)(2,1)S(1)} %or_select_fusion), channel_id=1, source_target_pairs={{8,0},{16,8},{24,16},{32,24},{40,32},{48,40},{56,48},{64,56},{72,6... | collective-permute-start | bytes 912392 | tf_op jit(solution)/shard_map/ppermute | solution.py:13
  35.9 1.2 copy-start.1
  102.6 32.5 %copy-start.2 = (bf16[128,128]{1,0:T(8,128)(2,1)S(1)}, bf16[128,128]{1,0:T(8,128)(2,1)}, u32[]{:S(2)}) copy-start(bf16[128,128]{1,0:T(8,128)(2,1)} %param.7) | copy-start | bytes 98308
where the time goes:
time: 138 us; the launch traced here: 136 us
  blocking collectives  89.2 us (65%)
  starting transfers between devices  20.8 us (15%)
  waiting for transfers between devices  10.8 us (8%)
  matrix products  6.28 us (5%)
  local copies, waits for them, and re-layouts  6.18 us (4%)
  other arithmetic  2.12 us (2%)
    all_to_all x1, blocking collectives, local(): lax.all_to_all(projected.reshape(1, groups, per_group, 3 * chans), 'rows'...  57.4 us
    all_to_all x1, blocking collectives, attend_projected(): lax.all_to_all(context, 'rows', split_axis=0, concat_axis=1, tiled=True)  31.8 us
    ppermute x4, starting transfers between devices, from_behind(): return lax.ppermute(block, axis, route)  14.9 us
    ppermute x4, waiting for transfers between devices, from_behind(): return lax.ppermute(block, axis, route)  10.2 us
    ppermute x1, starting transfers between devices, padded(): lax.ppermute(lax.slice_in_dim(block, block.shape[dim] - width, None, axis...  4.66 us
    dot_general x9, matrix products, local(): jnp.dot(window, taps[3 * tap_t + tap_y], preferred_element_type=jnp.float32)  3.34 us
  transfers between devices with their start and end apart: 6, of which 4 were waited for; matrix products, arithmetic and copies ran while one was open for 1% of the time, Pallas kernels for 0%

commit v1 on v0

v1 whole, which is shorter than its diff:
```python
import jax
import jax.numpy as jnp
from jax import lax
from jax.experimental import pallas as pl
from jax.experimental.pallas import tpu as pltpu
from jax.sharding import PartitionSpec as P

MESH = pl.DeviceIdType.MESH
F32 = jnp.float32
BF16 = jnp.bfloat16
FRAMES = 32
CH = 128
HALVES = 2
OFFSETS = [s for d in range(1, 17) for s in ((d,) if d == 16 else (d, 32 - d))]
TAPS = ((0.375, 0.625), (0.125, 0.875), (0.875, 0.125), (0.625, 0.375))


def lerp(weights, a, b):
    return weights[0] * a + weights[1] * b


def spread(x):
    out = [lerp(TAPS[3], x[0], x[1])]
    for k in range(1, len(x) - 1):
        out.append(lerp(TAPS[0], x[k - 1], x[k]))
        out.append(lerp(TAPS[1], x[k - 1], x[k]))
        out.append(lerp(TAPS[2], x[k], x[k + 1]))
        out.append(lerp(TAPS[3], x[k], x[k + 1]))
    out.append(lerp(TAPS[0], x[-2], x[-1]))
    return out


def kernel(
    low_hbm, w_hbm, ain_hbm, aout_hbm, out,
    low, w, ain, aout, edge, hal, hband, ext, extw, got, gf, u, rf, snd,
    ld_sem, h_send, h_recv, in_send, in_recv, o_send, o_recv,
):
    place = lax.axis_index("rows")
    col = lax.axis_index("cols")
    band = place // FRAMES
    me = place % FRAMES
    base = band * FRAMES
    other = (1 - band) * FRAMES + me
    left = (col + 7) % 8
    right = (col + 1) % 8

    def load(k, src, dst):
        cp = pltpu.make_async_copy(src, dst, ld_sem.at[k])
        cp.start()
        return cp

    load_low = load(0, low_hbm, low)
    load_w = load(1, w_hbm, w)
    load_ain = load(2, ain_hbm, ain)
    load_aout = load(3, aout_hbm, aout)

    bar = pltpu.get_barrier_semaphore()
    near = ((place, left), (place, right), (other, col), (other, left), (other, right))
    for target in near:
        pl.semaphore_signal(bar, inc=1, device_id=target, device_id_type=MESH)
    for s in OFFSETS:
        pl.semaphore_signal(
            bar, inc=1, device_id=(base + (me + s) % FRAMES, col), device_id_type=MESH
        )
    load_low.wait()
    edge[0] = low[:, 0, :]
    edge[1] = low[:, 15, :]
    pl.semaphore_wait(bar, FRAMES - 1 + len(near))

    edge_row = (1 - band) * 3
    sends = (
        (edge.at[1], hal.at[0], (place, right)),
        (edge.at[0], hal.at[1], (place, left)),
        (edge.at[1], hal.at[2], (other, right)),
        (edge.at[0], hal.at[3], (other, left)),
        (low.at[edge_row], hband, (other, col)),
    )
    rims = []
    for k, (src, dst, target) in enumerate(sends):
        cp = pltpu.make_async_remote_copy(
            src_ref=src, dst_ref=dst, send_sem=h_send.at[k], recv_sem=h_recv.at[k],
            device_id=target, device_id_type=MESH,
        )
        cp.start()
        rims.append(cp)
    mine = low[...].astype(F32)
    ext[1:5, 1:17] = mine
    for cp in rims:
        cp.wait_recv()
    first = col == 0
    last = col == 7
    ext[1:5, 0:1] = jnp.where(first, mine[:, 0:1], hal[0].astype(F32).reshape(4, 1, CH))
    ext[1:5, 17:18] = jnp.where(last, mine[:, 15:16], hal[1].astype(F32).reshape(4, 1, CH))
    across = hband[...].astype(F32)
    cl = hal[2].astype(F32)
    cr = hal[3].astype(F32)
    upper = band == 0
    cl = jnp.where(upper, cl[0:1], cl[3:4])
    cr = jnp.where(upper, cr[0:1], cr[3:4])
    cl = jnp.where(first, across[0:1], cl)
    cr = jnp.where(last, across[15:16], cr)
    fill_row = jnp.where(upper, 5, 0)
    same_row = jnp.where(upper, 0, 5)
    copy_row = jnp.where(upper, 1, 4)
    ext[fill_row, 1:17] = across
    ext[fill_row, 0:1] = cl
    ext[fill_row, 17:18] = cr
    ext[same_row] = ext[copy_row]
    for j in range(8):
        extw[:, j] = ext[:, 2 * j : 2 * j + 4].astype(BF16)

    for s in OFFSETS:
        slot = (me + s) % FRAMES
        pltpu.make_async_remote_copy(
            src_ref=extw.at[pl.ds(slot // 8, 3), slot % 8], dst_ref=got.at[me],
            send_sem=in_send, recv_sem=in_recv,
            device_id=(base + slot, col), device_id_type=MESH,
        ).start()
    got[me] = extw[pl.ds(me // 8, 3), me % 8]
    pltpu.make_async_copy(got.at[pl.ds(0, 31)], got.at[pl.ds(0, 31)], in_recv).wait()

    for f in range(FRAMES):
        for k in range(3):
            gf[12 * f + 4 * k : 12 * f + 4 * k + 4] = got[f, k].astype(F32)
    grid = [[gf[pl.ds(4 * k + c, FRAMES, stride=12)] for c in range(4)] for k in range(3)]
    columns = [spread([grid[k][c] for k in range(3)]) for c in range(4)]
    patch_row = me // 8
    patch_col = me % 8
    keep_top = jnp.where(upper & (patch_row == 0), 0.0, 1.0).astype(F32)
    keep_bottom = jnp.where((band == 1) & (patch_row == 3), 0.0, 1.0).astype(F32)
    keep_left = jnp.where(first & (patch_col == 0), 0.0, 1.0).astype(F32)
    keep_right = jnp.where(last & (patch_col == 7), 0.0, 1.0).astype(F32)
    for y in range(6):
        row = spread([columns[c][y] for c in range(4)])
        for x in range(10):
            value = row[x]
            if y == 0:
                value = value * keep_top
            if y == 5:
                value = value * keep_bottom
            if x == 0:
                value = value * keep_left
            if x == 9:
                value = value * keep_right
            u[y, x] = value.astype(BF16)

    load_w.wait()
    load_ain.wait()
    load_aout.wait()

    pixels = 16
    rows = pixels * FRAMES
    frame_id = lax.broadcasted_iota(jnp.int32, (rows, CH), 0) % FRAMES
    lane = lax.broadcasted_iota(jnp.int32, (128, CH), 1)
    head0 = (lane < 64).astype(F32).astype(BF16)
    head1 = (lane >= 64).astype(F32).astype(BF16)
    ones = jnp.concatenate([head0, head1], axis=0)
    s_row = lax.broadcasted_iota(jnp.int32, (128, 256), 0) // FRAMES
    s_lane = lax.broadcasted_iota(jnp.int32, (128, 256), 1) % 128 // FRAMES
    same_pixel = s_row == s_lane

    for h in range(HALVES):
        lhs = jnp.concatenate(
            [
                u[2 * h + dy : 2 * h + dy + 2, dx : dx + 8].reshape(rows, CH)
                for dy in range(3)
                for dx in range(3)
            ],
            axis=1,
        )
        w01 = jnp.concatenate([w[0:1152], w[1152:2304]], axis=1)
        y01 = jnp.dot(lhs, w01, preferred_element_type=F32)
        y2 = jnp.dot(lhs, w[2304:3456], preferred_element_type=F32)
        before = jnp.where(frame_id == 0, 0.0, pltpu.roll(y01[:, :CH], 1, 0))
        after = jnp.where(frame_id == FRAMES - 1, 0.0, pltpu.roll(y2, rows - 1, 0))
        total = before + y01[:, CH:] + after
        centre = u[2 * h + 1 : 2 * h + 3, 1:9].reshape(rows, CH).astype(F32)
        feat = (centre + total / (1.0 + jnp.exp(-total))).astype(BF16)
        proj = jnp.dot(feat, ain[...], preferred_element_type=F32).astype(BF16)
        for g in range(4):
            part = proj[128 * g : 128 * g + 128]
            q = part[:, :CH]
            k = part[:, CH : 2 * CH]
            v = part[:, 2 * CH :]
            keys = jnp.concatenate([k * head0, k * head1], axis=0)
            scores = lax.dot_general(
                q, keys, (((1,), (1,)), ((), ())), preferred_element_type=F32
            )
            scores = jnp.where(same_pixel, scores * 0.125, -1e30)
            m0 = jnp.max(scores[:, :128], axis=1, keepdims=True)
            m1 = jnp.max(scores[:, 128:], axis=1, keepdims=True)
            expo = jnp.concatenate(
                [jnp.exp(scores[:, :128] - m0), jnp.exp(scores[:, 128:] - m1)], axis=1
            ).astype(BF16)
            values = jnp.concatenate([v * head0, v * head1], axis=0)
            summed = jnp.dot(
                expo, jnp.concatenate([values, ones], axis=1), preferred_element_type=F32
            )
            context = (summed[:, :CH] / summed[:, CH:]).astype(BF16)
            output = jnp.dot(context, aout[...], preferred_element_type=F32)
            rf[128 * g : 128 * g + 128] = feat[128 * g : 128 * g + 128].astype(F32) + output
        for f in range(FRAMES):
            snd[h, f] = rf[pl.ds(f, pixels, stride=FRAMES)].astype(BF16)
        for s in OFFSETS:
            frame = (me + s) % FRAMES
            pltpu.make_async_remote_copy(
                src_ref=snd.at[h, frame], dst_ref=out.at[me, h],
                send_sem=o_send.at[h], recv_sem=o_recv.at[h],
                device_id=(base + frame, col), device_id_type=MESH,
            ).start()
        out[me, h] = snd[h, me]

    for cp in rims:
        cp.wait_send()
    pltpu.make_async_copy(got.at[pl.ds(0, 31)], got.at[pl.ds(0, 31)], in_send).wait()
    for h in range(HALVES):
        block = snd.at[h, pl.ds(0, 31)]
        pltpu.make_async_copy(block, block, o_send.at[h]).wait()
        pltpu.make_async_copy(block, block, o_recv.at[h]).wait()


def local(low_frames, conv_weight, attn_in, attn_out):
    vmem = pltpu.VMEM
    dma = pltpu.SemaphoreType.DMA
    patches = pl.pallas_call(
        kernel,
        out_shape=jax.ShapeDtypeStruct((FRAMES, HALVES, 16, CH), BF16),
        in_specs=[pl.BlockSpec(memory_space=pl.ANY)] * 4,
        out_specs=pl.BlockSpec(memory_space=pltpu.VMEM),
        scratch_shapes=[
            vmem((4, 16, CH), BF16),
            vmem((27 * CH, CH), BF16),
            vmem((CH, 3 * CH), BF16),
            vmem((CH, CH), BF16),
            vmem((2, 4, CH), BF16),
            vmem((4, 4, CH), BF16),
            vmem((16, CH), BF16),
            vmem((6, 24, CH), F32),
            vmem((6, 8, 4, CH), BF16),
            vmem((FRAMES, 3, 4, CH), BF16),
            vmem((FRAMES * 12, CH), F32),
            vmem((6, 10, FRAMES, CH), BF16),
            vmem((16 * FRAMES, CH), F32),
            vmem((HALVES, FRAMES, 16, CH), BF16),
            dma((4,)),
            dma((5,)),
            dma((5,)),
            dma,
            dma,
            dma((HALVES,)),
            dma((HALVES,)),
        ],
        compiler_params=pltpu.CompilerParams(
            collective_id=0, has_side_effects=True, vmem_limit_bytes=32 * 1024 * 1024
        ),
    )(low_frames, conv_weight, attn_in, attn_out)
    blocks = patches.reshape(4, 8, 4, 8, CH)
    return jnp.transpose(blocks, (0, 2, 1, 3, 4)).reshape(16, 64, CH)


def solution(mesh):
    in_specs = (P("rows", "cols", None), P(), P(), P())
    out_specs = P("rows", "cols", None)
    return jax.shard_map(local, mesh=mesh, in_specs=in_specs, out_specs=out_specs, check_vma=False)
```

time: 138 us -> 54.9 us (0.40); the launches traced: 136 us -> 54.6 us
  blocking collectives: 89.2 us -> 0 us
  Pallas kernels: 0 us -> 50.3 us
  starting transfers between devices: 20.8 us -> 0 us
  waiting for transfers between devices: 10.8 us -> 0 us
  matrix products: 6.28 us -> 0 us
  other arithmetic: 2.12 us -> 0 us
  local copies, waits for them, and re-layouts: 6.18 us -> 4.3 us
    all_to_all x2 -> x0, blocking collectives: 89.2 us -> none  [the longest x1 57.4 us: local(): lax.all_to_all(projected.reshape(1, groups, per_group, 3 * chans), 'rows'...]
    pallas_call x0 -> x1, Pallas kernels: none -> 50.3 us  [local(): pl.pallas_call(kernel, out_shape=jax.ShapeDtypeStruct((FRAMES, HALVES, 16...]
    ppermute x6 -> x0, starting transfers between devices: 20.8 us -> none  [the longest x4 14.9 us: from_behind(): return lax.ppermute(block, axis, route)]
    ppermute x6 -> x0, waiting for transfers between devices: 10.8 us -> none  [the longest x4 10.2 us: from_behind(): return lax.ppermute(block, axis, route)]
    dot_general x13 -> x0, matrix products: 5.58 us -> none  [the longest x9 3.34 us: local(): jnp.dot(window, taps[3 * tap_t + tap_y], preferred_element_type=jnp.float32)]
    slice x5 -> x0, local copies, waits for them, and re-layouts: 2.6 us -> none  [the longest x3 1.43 us: local(): slabs[tap_t][tap_y:tap_y + rows_high, offset:offset + cols_high]]
    unnamed x7 -> x8, local copies, waits for them, and re-layouts: 1.82 us -> 3.53 us
  transfers between devices with their start and end apart: 6 -> 0, of which waited for: 4 -> 0; matrix products, arithmetic and copies ran while one was open for 1% -> 0% of each run, Pallas kernels for 0% -> 0%
where the time goes in v1:
time: 54.9 us; the launch traced here: 54.6 us
  Pallas kernels  50.3 us (92%)
  local copies, waits for them, and re-layouts  4.3 us (8%)
    pallas_call x1, Pallas kernels, local(): pl.pallas_call(kernel, out_shape=jax.ShapeDtypeStruct((FRAMES, HALVES, 16...  50.3 us
    unnamed x8, local copies, waits for them, and re-layouts  3.53 us

profile of v1, /device:TPU:1, one launch (start us, length us, event | category | flops | bytes accessed | tf_op | source)
XLA Modules:
  0.0 54.6 jit_solution(13957014565169930598)
XLA Ops:
  0.0 0.0 copy-start
  0.0 1.2 %copy-done = bf16[3456,128]{1,0:T(8,128)(2,1)S(1)} copy-done((bf16[3456,128]{1,0:T(8,128)(2,1)S(1)}, bf16[3456,128]{1,0:T(8,128)(2,1)}, u32[]{:S(2)}) %copy-start) | copy-done | bytes 884760
  1.2 0.0 copy-start.1
  1.2 0.9 %copy-done.1 = bf16[128,384]{1,0:T(8,128)(2,1)S(1)} copy-done((bf16[128,384]{1,0:T(8,128)(2,1)S(1)}, bf16[128,384]{1,0:T(8,128)(2,1)}, u32[]{:S(2)}) %copy-start.1) | copy-done | bytes 98328
  2.1 0.0 copy-start.2
  2.1 0.8 %copy-done.2 = bf16[128,128]{1,0:T(8,128)(2,1)S(1)} copy-done((bf16[128,128]{1,0:T(8,128)(2,1)S(1)}, bf16[128,128]{1,0:T(8,128)(2,1)}, u32[]{:S(2)}) %copy-start.2) | copy-done | bytes 32792
  2.8 0.0 copy-start.3
  2.8 0.7 %copy-done.3 = bf16[4,16,128]{2,1,0:T(8,128)(2,1)S(1)} copy-done((bf16[4,16,128]{2,1,0:T(8,128)(2,1)S(1)}, bf16[4,16,128]{2,1,0:T(8,128)(2,1)}, u32[]{:S(2)}) %copy-start.3) | copy-done | bytes 16408
  3.5 50.3 %shard_map.46 = bf16[32,2,16,128]{3,2,1,0:T(8,128)(2,1)S(1)} custom-call(bf16[4,16,128]{2,1,0:T(8,128)(2,1)S(1)} %copy-done.3, bf16[3456,128]{1,0:T(8,128)(2,1)S(1)} %copy-done, bf16[128,384]{1,0:T(8,128)(2,1)S(1)} %copy-done.1, bf16[128,128]{1,0:T(8,128)(2,1)S(1)} %copy-done.2), custom_call_target="tpu_custom_call" | custom-call | tf_op jit(solution)/shard_map/pallas_call | solution.py:225
  53.8 0.8 %copy.5 = bf16[4,4,8,8,128]{4,3,2,1,0:T(8,128)(2,1)} copy(bf16[4,4,8,8,128]{4,3,1,2,0:T(8,128)(2,1)S(1)} %bitcast.4) | data formatting | bytes 524288 | tf_op jit(solution)/shard_map/transpose | solution.py:258
Async XLA Ops:
  0.0 1.2 %copy-start = (bf16[3456,128]{1,0:T(8,128)(2,1)S(1)}, bf16[3456,128]{1,0:T(8,128)(2,1)}, u32[]{:S(2)}) copy-start(bf16[3456,128]{1,0:T(8,128)(2,1)} %w_hbm.1) | copy-start | bytes 2654212
  1.2 0.9 %copy-start.1 = (bf16[128,384]{1,0:T(8,128)(2,1)S(1)}, bf16[128,384]{1,0:T(8,128)(2,1)}, u32[]{:S(2)}) copy-start(bf16[128,384]{1,0:T(8,128)(2,1)} %ain_hbm.1) | copy-start | bytes 294916
  2.1 0.8 %copy-start.2 = (bf16[128,128]{1,0:T(8,128)(2,1)S(1)}, bf16[128,128]{1,0:T(8,128)(2,1)}, u32[]{:S(2)}) copy-start(bf16[128,128]{1,0:T(8,128)(2,1)} %aout_hbm.1) | copy-start | bytes 98308
  2.8 0.7 %copy-start.3 = (bf16[4,16,128]{2,1,0:T(8,128)(2,1)S(1)}, bf16[4,16,128]{2,1,0:T(8,128)(2,1)}, u32[]{:S(2)}) copy-start(bf16[4,16,128]{2,1,0:T(8,128)(2,1)} %low_hbm.1) | copy-start | bytes 49156

commit v2 on v1

--- a/solution.py
+++ b/solution.py
@@ -11,7 +11,7 @@
 FRAMES = 32
 CH = 128
 HALVES = 2
-OFFSETS = [s for d in range(1, 17) for s in ((d,) if d == 16 else (d, 32 - d))]
+OFFSETS = [s for d in range(16, 0, -1) for s in ((d,) if d == 16 else (d, 32 - d))]
 TAPS = ((0.375, 0.625), (0.125, 0.875), (0.875, 0.125), (0.625, 0.375))
 
 
@@ -30,19 +30,36 @@
     return out
 
 
+def patch_of(index, band):
+    rest = index - 14
+    depth = jnp.where(
+        index < 8, 0, jnp.where(index < 14, 1 + (index - 8) // 2, 1 + rest // 6)
+    )
+    column = jnp.where(
+        index < 8, index, jnp.where(index < 14, 7 * (index % 2), 1 + rest % 6)
+    )
+    return jnp.where(band == 0, 3 - depth, depth), column
+
+
 def kernel(
     low_hbm, w_hbm, ain_hbm, aout_hbm, out,
-    low, w, ain, aout, edge, hal, hband, ext, extw, got, gf, u, rf, snd,
-    ld_sem, h_send, h_recv, in_send, in_recv, o_send, o_recv,
+    low, w, ain, aout, edge, ext, extw, got, halo, gf, gh, u, rf, snd,
+    ld_sem, in_send, in_recv, h_send, h_recv, o_send, o_recv,
 ):
     place = lax.axis_index("rows")
     col = lax.axis_index("cols")
     band = place // FRAMES
     me = place % FRAMES
     base = band * FRAMES
-    other = (1 - band) * FRAMES + me
+    across = (1 - band) * FRAMES
     left = (col + 7) % 8
     right = (col + 1) % 8
+    patch_row, patch_col = patch_of(me, band)
+    patch = patch_row * 8 + patch_col
+    border = jnp.where(band == 0, 3, 0)
+    at_border = patch_row == border
+    at_left = patch_col == 0
+    at_right = patch_col == 7
 
     def load(k, src, dst):
         cp = pltpu.make_async_copy(src, dst, ld_sem.at[k])
@@ -55,81 +72,130 @@
     load_aout = load(3, aout_hbm, aout)
 
     bar = pltpu.get_barrier_semaphore()
-    near = ((place, left), (place, right), (other, col), (other, left), (other, right))
-    for target in near:
-        pl.semaphore_signal(bar, inc=1, device_id=target, device_id_type=MESH)
+
+    def tell(row, column):
+        pl.semaphore_signal(bar, inc=1, device_id=(row, column), device_id_type=MESH)
+
+    def tell_ring(ring, column):
+        def one(f, _):
+            tell(ring + f, column)
+            return _
+
+        lax.fori_loop(0, FRAMES, one, 0)
+
     for s in OFFSETS:
-        pl.semaphore_signal(
-            bar, inc=1, device_id=(base + (me + s) % FRAMES, col), device_id_type=MESH
-        )
+        tell(base + (me + s) % FRAMES, col)
+
+    @pl.when(at_left)
+    def _():
+        tell_ring(base, left)
+
+    @pl.when(at_right)
+    def _():
+        tell_ring(base, right)
+
+    @pl.when(at_border)
+    def _():
+        tell_ring(across, col)
+
+    @pl.when(at_border & at_left)
+    def _():
+        tell_ring(across, left)
+
+    @pl.when(at_border & at_right)
+    def _():
+        tell_ring(across, right)
+
     load_low.wait()
+    mine = low[...].astype(F32)
     edge[0] = low[:, 0, :]
     edge[1] = low[:, 15, :]
-    pl.semaphore_wait(bar, FRAMES - 1 + len(near))
-
-    edge_row = (1 - band) * 3
-    sends = (
-        (edge.at[1], hal.at[0], (place, right)),
-        (edge.at[0], hal.at[1], (place, left)),
-        (edge.at[1], hal.at[2], (other, right)),
-        (edge.at[0], hal.at[3], (other, left)),
-        (low.at[edge_row], hband, (other, col)),
-    )
-    rims = []
-    for k, (src, dst, target) in enumerate(sends):
-        cp = pltpu.make_async_remote_copy(
-            src_ref=src, dst_ref=dst, send_sem=h_send.at[k], recv_sem=h_recv.at[k],
-            device_id=target, device_id_type=MESH,
-        )
-        cp.start()
-        rims.append(cp)
-    mine = low[...].astype(F32)
     ext[1:5, 1:17] = mine
-    for cp in rims:
-        cp.wait_recv()
-    first = col == 0
-    last = col == 7
-    ext[1:5, 0:1] = jnp.where(first, mine[:, 0:1], hal[0].astype(F32).reshape(4, 1, CH))
-    ext[1:5, 17:18] = jnp.where(last, mine[:, 15:16], hal[1].astype(F32).reshape(4, 1, CH))
-    across = hband[...].astype(F32)
-    cl = hal[2].astype(F32)
-    cr = hal[3].astype(F32)
-    upper = band == 0
-    cl = jnp.where(upper, cl[0:1], cl[3:4])
-    cr = jnp.where(upper, cr[0:1], cr[3:4])
-    cl = jnp.where(first, across[0:1], cl)
-    cr = jnp.where(last, across[15:16], cr)
-    fill_row = jnp.where(upper, 5, 0)
-    same_row = jnp.where(upper, 0, 5)
-    copy_row = jnp.where(upper, 1, 4)
-    ext[fill_row, 1:17] = across
-    ext[fill_row, 0:1] = cl
-    ext[fill_row, 17:18] = cr
-    ext[same_row] = ext[copy_row]
+    ext[1:5, 0:1] = mine[:, 0:1]
+    ext[1:5, 17:18] = mine[:, 15:16]
+    ext[0] = ext[1]
+    ext[5] = ext[4]
     for j in range(8):
         extw[:, j] = ext[:, 2 * j : 2 * j + 4].astype(BF16)
+    pl.semaphore_wait(bar, FRAMES - 1 + 18)
 
     for s in OFFSETS:
-        slot = (me + s) % FRAMES
+        to = (me + s) % FRAMES
+        r, j = patch_of(to, band)
         pltpu.make_async_remote_copy(
-            src_ref=extw.at[pl.ds(slot // 8, 3), slot % 8], dst_ref=got.at[me],
+            src_ref=extw.at[pl.ds(r, 3), j], dst_ref=got.at[me],
             send_sem=in_send, recv_sem=in_recv,
-            device_id=(base + slot, col), device_id_type=MESH,
+            device_id=(base + to, col), device_id_type=MESH,
         ).start()
-    got[me] = extw[pl.ds(me // 8, 3), me % 8]
+
+    def rim(src, kind, to, column):
+        pltpu.make_async_remote_copy(
+            src_ref=src, dst_ref=halo.at[kind, me], send_sem=h_send, recv_sem=h_recv.at[kind],
+            device_id=(to, column), device_id_type=MESH,
+        ).start()
+
+    for to in (0, 8, 10, 12):
+        rim(edge.at[1], 0, base + to, right)
+    for to in (7, 9, 11, 13):
+        rim(edge.at[0], 1, base + to, left)
+    for to in range(8):
+        rim(extw.at[border + 1, to], 2, across + to, col)
+    rim(edge.at[1], 3, across, right)
+    rim(edge.at[0], 4, across + 7, left)
+    got[me] = extw[pl.ds(patch_row, 3), patch_col]
+
     pltpu.make_async_copy(got.at[pl.ds(0, 31)], got.at[pl.ds(0, 31)], in_recv).wait()
-
     for f in range(FRAMES):
         for k in range(3):
             gf[12 * f + 4 * k : 12 * f + 4 * k + 4] = got[f, k].astype(F32)
+
+    def take(kind):
+        pltpu.make_async_copy(halo.at[kind], halo.at[kind], h_recv.at[kind]).wait()
+        for f in range(FRAMES):
+            gh[4 * f : 4 * f + 4] = halo[kind, f].astype(F32)
+
+    border_row = jnp.where(band == 0, 2, 0)
+    other_row = jnp.where(band == 0, 0, 3)
+
+    @pl.when(at_border)
+    def _():
+        take(2)
+        for c in range(4):
+            gf[pl.ds(4 * border_row + c, FRAMES, stride=12)] = gh[pl.ds(c, FRAMES, stride=4)]
+
+    def side(kind, c, inside):
+        take(kind)
+
+        @pl.when(inside)
+        def _():
+            for k in range(3):
+                r = jnp.clip(patch_row - 1 + k, 0, 3)
+                gf[pl.ds(4 * k + c, FRAMES, stride=12)] = gh[pl.ds(r, FRAMES, stride=4)]
+
+        @pl.when(at_border)
+        def _():
+            take(kind + 3)
+
+            @pl.when(inside)
+            def _():
+                gf[pl.ds(4 * border_row + c, FRAMES, stride=12)] = gh[
+                    pl.ds(other_row, FRAMES, stride=4)
+                ]
+
+    @pl.when(at_left)
+    def _():
+        side(0, 0, col > 0)
+
+    @pl.when(at_right)
+    def _():
+        side(1, 3, col < 7)
+
     grid = [[gf[pl.ds(4 * k + c, FRAMES, stride=12)] for c in range(4)] for k in range(3)]
     columns = [spread([grid[k][c] for k in range(3)]) for c in range(4)]
-    patch_row = me // 8
-    patch_col = me % 8
-    keep_top = jnp.where(upper & (patch_row == 0), 0.0, 1.0).astype(F32)
+    keep_top = jnp.where((band == 0) & (patch_row == 0), 0.0, 1.0).astype(F32)
     keep_bottom = jnp.where((band == 1) & (patch_row == 3), 0.0, 1.0).astype(F32)
-    keep_left = jnp.where(first & (patch_col == 0), 0.0, 1.0).astype(F32)
-    keep_right = jnp.where(last & (patch_col == 7), 0.0, 1.0).astype(F32)
+    keep_left = jnp.where((col == 0) & at_left, 0.0, 1.0).astype(F32)
+    keep_right = jnp.where((col == 7) & at_right, 0.0, 1.0).astype(F32)
     for y in range(6):
         row = spread([columns[c][y] for c in range(4)])
         for x in range(10):
@@ -204,14 +270,14 @@
         for s in OFFSETS:
             frame = (me + s) % FRAMES
             pltpu.make_async_remote_copy(
-                src_ref=snd.at[h, frame], dst_ref=out.at[me, h],
+                src_ref=snd.at[h, frame], dst_ref=out.at[patch, h],
                 send_sem=o_send.at[h], recv_sem=o_recv.at[h],
                 device_id=(base + frame, col), device_id_type=MESH,
             ).start()
-        out[me, h] = snd[h, me]
-
-    for cp in rims:
-        cp.wait_send()
+        out[patch, h] = snd[h, me]
+
+    sent = halo.at[0, pl.ds(0, 18)]
+    pltpu.make_async_copy(sent, sent, h_send).wait()
     pltpu.make_async_copy(got.at[pl.ds(0, 31)], got.at[pl.ds(0, 31)], in_send).wait()
     for h in range(HALVES):
         block = snd.at[h, pl.ds(0, 31)]
@@ -233,25 +299,25 @@
             vmem((CH, 3 * CH), BF16),
             vmem((CH, CH), BF16),
             vmem((2, 4, CH), BF16),
-            vmem((4, 4, CH), BF16),
-            vmem((16, CH), BF16),
             vmem((6, 24, CH), F32),
             vmem((6, 8, 4, CH), BF16),
             vmem((FRAMES, 3, 4, CH), BF16),
+            vmem((5, FRAMES, 4, CH), BF16),
             vmem((FRAMES * 12, CH), F32),
+            vmem((FRAMES * 4, CH), F32),
             vmem((6, 10, FRAMES, CH), BF16),
             vmem((16 * FRAMES, CH), F32),
             vmem((HALVES, FRAMES, 16, CH), BF16),
             dma((4,)),
-            dma((5,)),
-            dma((5,)),
             dma,
             dma,
+            dma,
+            dma((5,)),
             dma((HALVES,)),
             dma((HALVES,)),
         ],
         compiler_params=pltpu.CompilerParams(
-            collective_id=0, has_side_effects=True, vmem_limit_bytes=32 * 1024 * 1024
+            collective_id=0, has_side_effects=True, vmem_limit_bytes=56 * 1024 * 1024
         ),
     )(low_frames, conv_weight, attn_in, attn_out)
     blocks = patches.reshape(4, 8, 4, 8, CH)

time: 54.9 us -> 46.6 us (0.85)
  Pallas kernels: 50.3 us -> 44.7 us
  local copies, waits for them, and re-layouts: 4.3 us -> 1.72 us
    pallas_call x1, Pallas kernels: 50.3 us -> 44.7 us  [local(): pl.pallas_call(kernel, out_shape=jax.ShapeDtypeStruct((FRAMES, HALVES, 16...]
    unnamed x8 -> x0, local copies, waits for them, and re-layouts: 3.53 us -> none
    transpose x1, local copies, waits for them, and re-layouts: 0.77 us -> 1.72 us  [local(): return jnp.transpose(blocks, (0, 2, 1, 3, 4)).reshape(16, 64, CH)]
where the time goes in v2:
time: 46.6 us; the launch traced here: 46.4 us
  Pallas kernels  44.7 us (96%)
  local copies, waits for them, and re-layouts  1.72 us (4%)
    pallas_call x1, Pallas kernels, local(): pl.pallas_call(kernel, out_shape=jax.ShapeDtypeStruct((FRAMES, HALVES, 16...  44.7 us
    transpose x1, local copies, waits for them, and re-layouts, local(): return jnp.transpose(blocks, (0, 2, 1, 3, 4)).reshape(16, 64, CH)  1.72 us

profile of v2, /device:TPU:1, one launch (start us, length us, event | category | flops | bytes accessed | tf_op | source)
XLA Modules:
  0.0 46.4 jit_solution(6843726009648046187)
XLA Ops:
  0.0 44.7 %shard_map.46 = bf16[32,2,16,128]{3,2,1,0:T(8,128)(2,1)} custom-call(bf16[4,16,128]{2,1,0:T(8,128)(2,1)} %low_hbm.1, bf16[3456,128]{1,0:T(8,128)(2,1)} %w_hbm.1, bf16[128,384]{1,0:T(8,128)(2,1)} %ain_hbm.1, bf16[128,128]{1,0:T(8,128)(2,1)} %aout_hbm.1), custom_call_target="tpu_custom_call" | custom-call | tf_op jit(solution)/shard_map/pallas_call | solution.py:291
  44.7 1.7 %copy.5 = bf16[4,4,8,8,128]{4,3,2,1,0:T(8,128)(2,1)} copy(bf16[4,4,8,8,128]{4,3,1,2,0:T(8,128)(2,1)} %bitcast.4) | data formatting | bytes 524288 | tf_op jit(solution)/shard_map/transpose | solution.py:324

commit v3 on v2

--- a/solution.py
+++ b/solution.py
@@ -9,8 +9,11 @@
 F32 = jnp.float32
 BF16 = jnp.bfloat16
 FRAMES = 32
+EARLY = 16
+GROUP_OFFSETS = [s for d in range(8, 0, -1) for s in ((d,) if d == 8 else (d, 16 - d))]
+ACROSS_OFFSETS = [0] + GROUP_OFFSETS[::-1]
 CH = 128
-HALVES = 2
+PIECES = ((0, 1), (1, 4))
 OFFSETS = [s for d in range(16, 0, -1) for s in ((d,) if d == 16 else (d, 32 - d))]
 TAPS = ((0.375, 0.625), (0.125, 0.875), (0.875, 0.125), (0.625, 0.375))
 
@@ -119,8 +122,7 @@
         extw[:, j] = ext[:, 2 * j : 2 * j + 4].astype(BF16)
     pl.semaphore_wait(bar, FRAMES - 1 + 18)
 
-    for s in OFFSETS:
-        to = (me + s) % FRAMES
+    def window(to):
         r, j = patch_of(to, band)
         pltpu.make_async_remote_copy(
             src_ref=extw.at[pl.ds(r, 3), j], dst_ref=got.at[me],
@@ -134,14 +136,34 @@
             device_id=(to, column), device_id_type=MESH,
         ).start()
 
-    for to in (0, 8, 10, 12):
-        rim(edge.at[1], 0, base + to, right)
-    for to in (7, 9, 11, 13):
-        rim(edge.at[0], 1, base + to, left)
-    for to in range(8):
-        rim(extw.at[border + 1, to], 2, across + to, col)
-    rim(edge.at[1], 3, across, right)
-    rim(edge.at[0], 4, across + 7, left)
+    def rims():
+        for to in (0, 8, 10, 12):
+            rim(edge.at[1], 0, base + to, right)
+        for to in (7, 9, 11, 13):
+            rim(edge.at[0], 1, base + to, left)
+        for to in range(8):
+            rim(extw.at[border + 1, to], 2, across + to, col)
+        rim(edge.at[1], 3, across, right)
+        rim(edge.at[0], 4, across + 7, left)
+
+    early = me < EARLY
+
+    @pl.when(early)
+    def _():
+        for s in ACROSS_OFFSETS:
+            window(EARLY + (me + s) % EARLY)
+        rims()
+        for s in GROUP_OFFSETS:
+            window((me + s) % EARLY)
+
+    @pl.when(jnp.logical_not(early))
+    def _():
+        for s in GROUP_OFFSETS:
+            window(EARLY + (me + s) % EARLY)
+        rims()
+        for s in ACROSS_OFFSETS:
+            window((me + s) % EARLY)
+
     got[me] = extw[pl.ds(patch_row, 3), patch_col]
 
     pltpu.make_async_copy(got.at[pl.ds(0, 31)], got.at[pl.ds(0, 31)], in_recv).wait()
@@ -214,9 +236,6 @@
     load_ain.wait()
     load_aout.wait()
 
-    pixels = 16
-    rows = pixels * FRAMES
-    frame_id = lax.broadcasted_iota(jnp.int32, (rows, CH), 0) % FRAMES
     lane = lax.broadcasted_iota(jnp.int32, (128, CH), 1)
     head0 = (lane < 64).astype(F32).astype(BF16)
     head1 = (lane >= 64).astype(F32).astype(BF16)
@@ -225,10 +244,24 @@
     s_lane = lax.broadcasted_iota(jnp.int32, (128, 256), 1) % 128 // FRAMES
     same_pixel = s_row == s_lane
 
-    for h in range(HALVES):
+    def give(h, frame):
+        top, bottom = PIECES[h]
+
+        @pl.when(frame != me)
+        def _():
+            pltpu.make_async_remote_copy(
+                src_ref=snd.at[frame, top:bottom], dst_ref=out.at[patch, top:bottom],
+                send_sem=o_send.at[h], recv_sem=o_recv.at[h],
+                device_id=(base + frame, col), device_id_type=MESH,
+            ).start()
+
+    for h, (top, bottom) in enumerate(PIECES):
+        pixels = 8 * (bottom - top)
+        rows = pixels * FRAMES
+        frame_id = lax.broadcasted_iota(jnp.int32, (rows, CH), 0) % FRAMES
         lhs = jnp.concatenate(
             [
-                u[2 * h + dy : 2 * h + dy + 2, dx : dx + 8].reshape(rows, CH)
+                u[top + dy : bottom + dy, dx : dx + 8].reshape(rows, CH)
                 for dy in range(3)
                 for dx in range(3)
             ],
@@ -240,10 +273,10 @@
         before = jnp.where(frame_id == 0, 0.0, pltpu.roll(y01[:, :CH], 1, 0))
         after = jnp.where(frame_id == FRAMES - 1, 0.0, pltpu.roll(y2, rows - 1, 0))
         total = before + y01[:, CH:] + after
-        centre = u[2 * h + 1 : 2 * h + 3, 1:9].reshape(rows, CH).astype(F32)
+        centre = u[top + 1 : bottom + 1, 1:9].reshape(rows, CH).astype(F32)
         feat = (centre + total / (1.0 + jnp.exp(-total))).astype(BF16)
         proj = jnp.dot(feat, ain[...], preferred_element_type=F32).astype(BF16)
-        for g in range(4):
+        for g in range(rows // 128):
             part = proj[128 * g : 128 * g + 128]
             q = part[:, :CH]
             k = part[:, CH : 2 * CH]
@@ -266,21 +299,18 @@
             output = jnp.dot(context, aout[...], preferred_element_type=F32)
             rf[128 * g : 128 * g + 128] = feat[128 * g : 128 * g + 128].astype(F32) + output
         for f in range(FRAMES):
-            snd[h, f] = rf[pl.ds(f, pixels, stride=FRAMES)].astype(BF16)
-        for s in OFFSETS:
-            frame = (me + s) % FRAMES
-            pltpu.make_async_remote_copy(
-                src_ref=snd.at[h, frame], dst_ref=out.at[patch, h],
-                send_sem=o_send.at[h], recv_sem=o_recv.at[h],
-                device_id=(base + frame, col), device_id_type=MESH,
-            ).start()
-        out[patch, h] = snd[h, me]
+            for y in range(bottom - top):
+                snd[f, top + y] = rf[pl.ds(256 * y + f, 8, stride=FRAMES)].astype(BF16)
+        for lo in (0, EARLY):
+            for s in range(EARLY):
+                give(h, lo + (me + s) % EARLY)
+        out[patch, top:bottom] = snd[me, top:bottom]
 
     sent = halo.at[0, pl.ds(0, 18)]
     pltpu.make_async_copy(sent, sent, h_send).wait()
     pltpu.make_async_copy(got.at[pl.ds(0, 31)], got.at[pl.ds(0, 31)], in_send).wait()
-    for h in range(HALVES):
-        block = snd.at[h, pl.ds(0, 31)]
+    for h, (top, bottom) in enumerate(PIECES):
+        block = snd.at[pl.ds(0, 31), top:bottom]
         pltpu.make_async_copy(block, block, o_send.at[h]).wait()
         pltpu.make_async_copy(block, block, o_recv.at[h]).wait()
 
@@ -290,7 +320,7 @@
     dma = pltpu.SemaphoreType.DMA
     patches = pl.pallas_call(
         kernel,
-        out_shape=jax.ShapeDtypeStruct((FRAMES, HALVES, 16, CH), BF16),
+        out_shape=jax.ShapeDtypeStruct((FRAMES, 4, 8, CH), BF16),
         in_specs=[pl.BlockSpec(memory_space=pl.ANY)] * 4,
         out_specs=pl.BlockSpec(memory_space=pltpu.VMEM),
         scratch_shapes=[
@@ -306,15 +336,15 @@
             vmem((FRAMES * 12, CH), F32),
             vmem((FRAMES * 4, CH), F32),
             vmem((6, 10, FRAMES, CH), BF16),
-            vmem((16 * FRAMES, CH), F32),
-            vmem((HALVES, FRAMES, 16, CH), BF16),
+            vmem((32 * FRAMES, CH), F32),
+            vmem((FRAMES, 4, 8, CH), BF16),
             dma((4,)),
             dma,
             dma,
             dma,
             dma((5,)),
-            dma((HALVES,)),
-            dma((HALVES,)),
+            dma((len(PIECES),)),
+            dma((len(PIECES),)),
         ],
         compiler_params=pltpu.CompilerParams(
             collective_id=0, has_side_effects=True, vmem_limit_bytes=56 * 1024 * 1024

time: 46.6 us -> 43 us (0.923)
  Pallas kernels: 44.7 us -> 41.1 us
    pallas_call x1, Pallas kernels: 44.7 us -> 41.1 us  [local(): pl.pallas_call(kernel, out_shape=jax.ShapeDtypeStruct((FRAMES, 4, 8, CH),...]
where the time goes in v3:
time: 43 us; the launch traced here: 42.9 us
  Pallas kernels  41.1 us (96%)
  local copies, waits for them, and re-layouts  1.72 us (4%)
    pallas_call x1, Pallas kernels, local(): pl.pallas_call(kernel, out_shape=jax.ShapeDtypeStruct((FRAMES, 4, 8, CH),...  41.1 us
    transpose x1, local copies, waits for them, and re-layouts, local(): return jnp.transpose(blocks, (0, 2, 1, 3, 4)).reshape(16, 64, CH)  1.72 us

profile of v3, /device:TPU:1, one launch (start us, length us, event | category | flops | bytes accessed | tf_op | source)
XLA Modules:
  0.0 42.9 jit_solution(16624900272928497042)
XLA Ops:
  0.0 41.1 %shard_map.46 = bf16[32,4,8,128]{3,2,1,0:T(8,128)(2,1)} custom-call(bf16[4,16,128]{2,1,0:T(8,128)(2,1)} %low_hbm.1, bf16[3456,128]{1,0:T(8,128)(2,1)} %w_hbm.1, bf16[128,384]{1,0:T(8,128)(2,1)} %ain_hbm.1, bf16[128,128]{1,0:T(8,128)(2,1)} %aout_hbm.1), custom_call_target="tpu_custom_call" | custom-call | tf_op jit(solution)/shard_map/pallas_call | solution.py:321
  41.1 1.7 %copy.5 = bf16[4,4,8,8,128]{4,3,2,1,0:T(8,128)(2,1)} copy(bf16[4,4,8,8,128]{4,3,1,2,0:T(8,128)(2,1)} %bitcast.4) | data formatting | bytes 524288 | tf_op jit(solution)/shard_map/transpose | solution.py:354

commit v4 on v3

--- a/solution.py
+++ b/solution.py
@@ -13,6 +13,7 @@
 GROUP_OFFSETS = [s for d in range(8, 0, -1) for s in ((d,) if d == 8 else (d, 16 - d))]
 ACROSS_OFFSETS = [0] + GROUP_OFFSETS[::-1]
 CH = 128
+PARTS = ((0, 2), (2, 3))
 PIECES = ((0, 1), (1, 4))
 OFFSETS = [s for d in range(16, 0, -1) for s in ((d,) if d == 16 else (d, 32 - d))]
 TAPS = ((0.375, 0.625), (0.125, 0.875), (0.875, 0.125), (0.625, 0.375))
@@ -122,11 +123,12 @@
         extw[:, j] = ext[:, 2 * j : 2 * j + 4].astype(BF16)
     pl.semaphore_wait(bar, FRAMES - 1 + 18)
 
-    def window(to):
+    def window(to, part):
+        lo, hi = PARTS[part]
         r, j = patch_of(to, band)
         pltpu.make_async_remote_copy(
-            src_ref=extw.at[pl.ds(r, 3), j], dst_ref=got.at[me],
-            send_sem=in_send, recv_sem=in_recv,
+            src_ref=extw.at[pl.ds(r + lo, hi - lo), j], dst_ref=got.at[me, lo:hi],
+            send_sem=in_send, recv_sem=in_recv.at[part],
             device_id=(base + to, col), device_id_type=MESH,
         ).start()
 
@@ -150,87 +152,96 @@
 
     @pl.when(early)
     def _():
-        for s in ACROSS_OFFSETS:
-            window(EARLY + (me + s) % EARLY)
-        rims()
-        for s in GROUP_OFFSETS:
-            window((me + s) % EARLY)
+        for part in range(2):
+            for s in ACROSS_OFFSETS:
+                window(EARLY + (me + s) % EARLY, part)
+            if part == 0:
+                rims()
+            for s in GROUP_OFFSETS:
+                window((me + s) % EARLY, part)
 
     @pl.when(jnp.logical_not(early))
     def _():
-        for s in GROUP_OFFSETS:
-            window(EARLY + (me + s) % EARLY)
-        rims()
-        for s in ACROSS_OFFSETS:
-            window((me + s) % EARLY)
+        for part in range(2):
+            for s in GROUP_OFFSETS:
+                window(EARLY + (me + s) % EARLY, part)
+            if part == 0:
+                rims()
+            for s in ACROSS_OFFSETS:
+                window((me + s) % EARLY, part)
 
     got[me] = extw[pl.ds(patch_row, 3), patch_col]
-
-    pltpu.make_async_copy(got.at[pl.ds(0, 31)], got.at[pl.ds(0, 31)], in_recv).wait()
-    for f in range(FRAMES):
-        for k in range(3):
-            gf[12 * f + 4 * k : 12 * f + 4 * k + 4] = got[f, k].astype(F32)
-
-    def take(kind):
-        pltpu.make_async_copy(halo.at[kind], halo.at[kind], h_recv.at[kind]).wait()
-        for f in range(FRAMES):
-            gh[4 * f : 4 * f + 4] = halo[kind, f].astype(F32)
 
     border_row = jnp.where(band == 0, 2, 0)
     other_row = jnp.where(band == 0, 0, 3)
-
-    @pl.when(at_border)
-    def _():
-        take(2)
-        for c in range(4):
-            gf[pl.ds(4 * border_row + c, FRAMES, stride=12)] = gh[pl.ds(c, FRAMES, stride=4)]
-
-    def side(kind, c, inside):
-        take(kind)
-
-        @pl.when(inside)
+    sides = ((0, 0, at_left, col > 0), (1, 3, at_right, col < 7))
+
+    def take(kind, wanted):
+        @pl.when(wanted)
         def _():
-            for k in range(3):
-                r = jnp.clip(patch_row - 1 + k, 0, 3)
-                gf[pl.ds(4 * k + c, FRAMES, stride=12)] = gh[pl.ds(r, FRAMES, stride=4)]
-
-        @pl.when(at_border)
+            pltpu.make_async_copy(halo.at[kind], halo.at[kind], h_recv.at[kind]).wait()
+            for f in range(FRAMES):
+                gh[kind, 4 * f : 4 * f + 4] = halo[kind, f].astype(F32)
+
+    def arrive(part):
+        lo, hi = PARTS[part]
+        block = got.at[pl.ds(0, 31), lo:hi]
+        pltpu.make_async_copy(block, block, in_recv.at[part]).wait()
+        for f in range(FRAMES):
+            for k in range(lo, hi):
+                gf[12 * f + 4 * k : 12 * f + 4 * k + 4] = got[f, k].astype(F32)
+        has_border = at_border & (band == 1 - part)
+
+        @pl.when(has_border)
         def _():
-            take(kind + 3)
-
-            @pl.when(inside)
+            for c in range(4):
+                gf[pl.ds(4 * border_row + c, FRAMES, stride=12)] = gh[
+                    2, pl.ds(c, FRAMES, stride=4)
+                ]
+
+        for kind, c, at_side, inside in sides:
+
+            @pl.when(at_side & inside)
+            def _():
+                for k in range(lo, hi):
+                    r = jnp.clip(patch_row - 1 + k, 0, 3)
+                    gf[pl.ds(4 * k + c, FRAMES, stride=12)] = gh[
+                        kind, pl.ds(r, FRAMES, stride=4)
+                    ]
+
+            @pl.when(at_side & inside & has_border)
             def _():
                 gf[pl.ds(4 * border_row + c, FRAMES, stride=12)] = gh[
-                    pl.ds(other_row, FRAMES, stride=4)
+                    kind + 3, pl.ds(other_row, FRAMES, stride=4)
                 ]
 
-    @pl.when(at_left)
-    def _():
-        side(0, 0, col > 0)
-
-    @pl.when(at_right)
-    def _():
-        side(1, 3, col < 7)
-
-    grid = [[gf[pl.ds(4 * k + c, FRAMES, stride=12)] for c in range(4)] for k in range(3)]
-    columns = [spread([grid[k][c] for k in range(3)]) for c in range(4)]
     keep_top = jnp.where((band == 0) & (patch_row == 0), 0.0, 1.0).astype(F32)
     keep_bottom = jnp.where((band == 1) & (patch_row == 3), 0.0, 1.0).astype(F32)
     keep_left = jnp.where((col == 0) & at_left, 0.0, 1.0).astype(F32)
     keep_right = jnp.where((col == 7) & at_right, 0.0, 1.0).astype(F32)
-    for y in range(6):
-        row = spread([columns[c][y] for c in range(4)])
-        for x in range(10):
-            value = row[x]
-            if y == 0:
-                value = value * keep_top
-            if y == 5:
-                value = value * keep_bottom
-            if x == 0:
-                value = value * keep_left
-            if x == 9:
-                value = value * keep_right
-            u[y, x] = value.astype(BF16)
+    def lift(k, lines):
+        two = [[gf[pl.ds(4 * i + c, FRAMES, stride=12)] for c in range(4)] for i in (k, k + 1)]
+        for y, taps in lines:
+            row = spread([lerp(taps, two[0][c], two[1][c]) for c in range(4)])
+            for x in range(10):
+                value = row[x]
+                if y == 0:
+                    value = value * keep_top
+                if y == 5:
+                    value = value * keep_bottom
+                if x == 0:
+                    value = value * keep_left
+                if x == 9:
+                    value = value * keep_right
+                u[y, x] = value.astype(BF16)
+
+    take(0, at_left)
+    take(1, at_right)
+    take(2, at_border)
+    take(3, at_border & at_left)
+    take(4, at_border & at_right)
+    arrive(0)
+    lift(0, ((0, TAPS[3]), (1, TAPS[0]), (2, TAPS[1])))
 
     load_w.wait()
     load_ain.wait()
@@ -255,7 +266,11 @@
                 device_id=(base + frame, col), device_id_type=MESH,
             ).start()
 
+    own = []
     for h, (top, bottom) in enumerate(PIECES):
+        if h == 1:
+            arrive(1)
+            lift(1, ((3, TAPS[2]), (4, TAPS[3]), (5, TAPS[0])))
         pixels = 8 * (bottom - top)
         rows = pixels * FRAMES
         frame_id = lax.broadcasted_iota(jnp.int32, (rows, CH), 0) % FRAMES
@@ -304,7 +319,7 @@
         for lo in (0, EARLY):
             for s in range(EARLY):
                 give(h, lo + (me + s) % EARLY)
-        out[patch, top:bottom] = snd[me, top:bottom]
+        own.append(load(4 + h, snd.at[me, top:bottom], out.at[patch, top:bottom]))
 
     sent = halo.at[0, pl.ds(0, 18)]
     pltpu.make_async_copy(sent, sent, h_send).wait()
@@ -313,6 +328,7 @@
         block = snd.at[pl.ds(0, 31), top:bottom]
         pltpu.make_async_copy(block, block, o_send.at[h]).wait()
         pltpu.make_async_copy(block, block, o_recv.at[h]).wait()
+        own[h].wait()
 
 
 def local(low_frames, conv_weight, attn_in, attn_out):
@@ -322,7 +338,7 @@
         kernel,
         out_shape=jax.ShapeDtypeStruct((FRAMES, 4, 8, CH), BF16),
         in_specs=[pl.BlockSpec(memory_space=pl.ANY)] * 4,
-        out_specs=pl.BlockSpec(memory_space=pltpu.VMEM),
+        out_specs=pl.BlockSpec(memory_space=pl.ANY),
         scratch_shapes=[
             vmem((4, 16, CH), BF16),
             vmem((27 * CH, CH), BF16),
@@ -334,13 +350,13 @@
             vmem((FRAMES, 3, 4, CH), BF16),
             vmem((5, FRAMES, 4, CH), BF16),
             vmem((FRAMES * 12, CH), F32),
-            vmem((FRAMES * 4, CH), F32),
+            vmem((5, FRAMES * 4, CH), F32),
             vmem((6, 10, FRAMES, CH), BF16),
             vmem((32 * FRAMES, CH), F32),
             vmem((FRAMES, 4, 8, CH), BF16),
-            dma((4,)),
+            dma((4 + len(PIECES),)),
             dma,
-            dma,
+            dma((2,)),
             dma,
             dma((5,)),
             dma((len(PIECES),)),

time: 43 us -> 42 us (0.977)
  Pallas kernels: 41.1 us -> 40.1 us
    pallas_call x1, Pallas kernels: 41.1 us -> 40.1 us  [local(): pl.pallas_call(kernel, out_shape=jax.ShapeDtypeStruct((FRAMES, 4, 8, CH),...]
where the time goes in v4:
time: 42 us; the launch traced here: 41.9 us
  Pallas kernels  40.1 us (95%)
  local copies, waits for them, and re-layouts  1.72 us (4%)
    pallas_call x1, Pallas kernels, local(): pl.pallas_call(kernel, out_shape=jax.ShapeDtypeStruct((FRAMES, 4, 8, CH),...  40.1 us
    transpose x1, local copies, waits for them, and re-layouts, local(): return jnp.transpose(blocks, (0, 2, 1, 3, 4)).reshape(16, 64, CH)  1.72 us

profile of v4, /device:TPU:1, one launch (start us, length us, event | category | flops | bytes accessed | tf_op | source)
XLA Modules:
  0.0 41.9 jit_solution(14739009680562517378)
XLA Ops:
  0.0 40.1 %shard_map.46 = bf16[32,4,8,128]{3,2,1,0:T(8,128)(2,1)} custom-call(bf16[4,16,128]{2,1,0:T(8,128)(2,1)} %low_hbm.1, bf16[3456,128]{1,0:T(8,128)(2,1)} %w_hbm.1, bf16[128,384]{1,0:T(8,128)(2,1)} %ain_hbm.1, bf16[128,128]{1,0:T(8,128)(2,1)} %aout_hbm.1), custom_call_target="tpu_custom_call" | custom-call | tf_op jit(solution)/shard_map/pallas_call | solution.py:337
  40.1 1.7 %copy.5 = bf16[4,4,8,8,128]{4,3,2,1,0:T(8,128)(2,1)} copy(bf16[4,4,8,8,128]{4,3,1,2,0:T(8,128)(2,1)} %bitcast.4) | data formatting | bytes 524288 | tf_op jit(solution)/shard_map/transpose | solution.py:370

commit v5 on v4

--- a/solution.py
+++ b/solution.py
@@ -153,10 +153,10 @@
     @pl.when(early)
     def _():
         for part in range(2):
+            if part == 0:
+                rims()
             for s in ACROSS_OFFSETS:
                 window(EARLY + (me + s) % EARLY, part)
-            if part == 0:
-                rims()
             for s in GROUP_OFFSETS:
                 window((me + s) % EARLY, part)
 

time: 42 us -> 41.5 us (0.988); the launches traced: 41.9 us -> 40.8 us
  Pallas kernels: 40.1 us -> 39 us
    pallas_call x1, Pallas kernels: 40.1 us -> 39 us  [local(): pl.pallas_call(kernel, out_shape=jax.ShapeDtypeStruct((FRAMES, 4, 8, CH),...]
where the time goes in v5:
time: 41.5 us; the launch traced here: 40.8 us
  Pallas kernels  39 us (94%)
  local copies, waits for them, and re-layouts  1.72 us (4%)
    pallas_call x1, Pallas kernels, local(): pl.pallas_call(kernel, out_shape=jax.ShapeDtypeStruct((FRAMES, 4, 8, CH),...  39 us
    transpose x1, local copies, waits for them, and re-layouts, local(): return jnp.transpose(blocks, (0, 2, 1, 3, 4)).reshape(16, 64, CH)  1.72 us

profile of v5, /device:TPU:1, one launch (start us, length us, event | category | flops | bytes accessed | tf_op | source)
XLA Modules:
  0.0 40.8 jit_solution(7782406987387175367)
XLA Ops:
  0.0 39.0 %shard_map.46 = bf16[32,4,8,128]{3,2,1,0:T(8,128)(2,1)} custom-call(bf16[4,16,128]{2,1,0:T(8,128)(2,1)} %low_hbm.1, bf16[3456,128]{1,0:T(8,128)(2,1)} %w_hbm.1, bf16[128,384]{1,0:T(8,128)(2,1)} %ain_hbm.1, bf16[128,128]{1,0:T(8,128)(2,1)} %aout_hbm.1), custom_call_target="tpu_custom_call" | custom-call | tf_op jit(solution)/shard_map/pallas_call | solution.py:337
  39.0 1.7 %copy.5 = bf16[4,4,8,8,128]{4,3,2,1,0:T(8,128)(2,1)} copy(bf16[4,4,8,8,128]{4,3,1,2,0:T(8,128)(2,1)} %bitcast.4) | data formatting | bytes 524288 | tf_op jit(solution)/shard_map/transpose | solution.py:370

commit v6 on v5

--- a/solution.py
+++ b/solution.py
@@ -318,7 +318,7 @@
                 snd[f, top + y] = rf[pl.ds(256 * y + f, 8, stride=FRAMES)].astype(BF16)
         for lo in (0, EARLY):
             for s in range(EARLY):
-                give(h, lo + (me + s) % EARLY)
+                give(h, lo + (me + 15 + s) % EARLY)
         own.append(load(4 + h, snd.at[me, top:bottom], out.at[patch, top:bottom]))
 
     sent = halo.at[0, pl.ds(0, 18)]
@@ -349,10 +349,10 @@
             vmem((6, 8, 4, CH), BF16),
             vmem((FRAMES, 3, 4, CH), BF16),
             vmem((5, FRAMES, 4, CH), BF16),
-            vmem((FRAMES * 12, CH), F32),
-            vmem((5, FRAMES * 4, CH), F32),
+            vmem((FRAMES * 12 + 16, CH), F32),
+            vmem((5, FRAMES * 4 + 8, CH), F32),
             vmem((6, 10, FRAMES, CH), BF16),
-            vmem((32 * FRAMES, CH), F32),
+            vmem((33 * FRAMES, CH), F32),
             vmem((FRAMES, 4, 8, CH), BF16),
             dma((4 + len(PIECES),)),
             dma,

time: 41.5 us -> 41.1 us (level); the launches traced: 40.8 us -> 40.8 us
  no operation moved by 1% of the time
where the time goes in v6:
time: 41.1 us; the launch traced here: 40.8 us
  Pallas kernels  39.1 us (95%)
  local copies, waits for them, and re-layouts  1.72 us (4%)
    pallas_call x1, Pallas kernels, local(): pl.pallas_call(kernel, out_shape=jax.ShapeDtypeStruct((FRAMES, 4, 8, CH),...  39.1 us
    transpose x1, local copies, waits for them, and re-layouts, local(): return jnp.transpose(blocks, (0, 2, 1, 3, 4)).reshape(16, 64, CH)  1.72 us

profile of v6, /device:TPU:1, one launch (start us, length us, event | category | flops | bytes accessed | tf_op | source)
XLA Modules:
  0.0 40.8 jit_solution(16521436773265047031)
XLA Ops:
  0.0 39.1 %shard_map.46 = bf16[32,4,8,128]{3,2,1,0:T(8,128)(2,1)} custom-call(bf16[4,16,128]{2,1,0:T(8,128)(2,1)} %low_hbm.1, bf16[3456,128]{1,0:T(8,128)(2,1)} %w_hbm.1, bf16[128,384]{1,0:T(8,128)(2,1)} %ain_hbm.1, bf16[128,128]{1,0:T(8,128)(2,1)} %aout_hbm.1), custom_call_target="tpu_custom_call" | custom-call | tf_op jit(solution)/shard_map/pallas_call | solution.py:337
  39.1 1.7 %copy.5 = bf16[4,4,8,8,128]{4,3,2,1,0:T(8,128)(2,1)} copy(bf16[4,4,8,8,128]{4,3,1,2,0:T(8,128)(2,1)} %bitcast.4) | data formatting | bytes 524288 | tf_op jit(solution)/shard_map/transpose | solution.py:370

commit v7 on v6

--- a/solution.py
+++ b/solution.py
@@ -71,9 +71,6 @@
         return cp
 
     load_low = load(0, low_hbm, low)
-    load_w = load(1, w_hbm, w)
-    load_ain = load(2, ain_hbm, ain)
-    load_aout = load(3, aout_hbm, aout)
 
     bar = pltpu.get_barrier_semaphore()
 
@@ -170,6 +167,9 @@
             for s in ACROSS_OFFSETS:
                 window((me + s) % EARLY, part)
 
+    load_w = load(1, w_hbm, w)
+    load_ain = load(2, ain_hbm, ain)
+    load_aout = load(3, aout_hbm, aout)
     got[me] = extw[pl.ds(patch_row, 3), patch_col]
 
     border_row = jnp.where(band == 0, 2, 0)

time: 41.1 us -> 41.1 us (level)
  no operation moved by 1% of the time
where the time goes in v7:
time: 41.1 us; the launch traced here: 40.8 us
  Pallas kernels  39.1 us (95%)
  local copies, waits for them, and re-layouts  1.72 us (4%)
    pallas_call x1, Pallas kernels, local(): pl.pallas_call(kernel, out_shape=jax.ShapeDtypeStruct((FRAMES, 4, 8, CH),...  39.1 us
    transpose x1, local copies, waits for them, and re-layouts, local(): return jnp.transpose(blocks, (0, 2, 1, 3, 4)).reshape(16, 64, CH)  1.72 us

profile of v7, /device:TPU:1, one launch (start us, length us, event | category | flops | bytes accessed | tf_op | source)
XLA Modules:
  0.0 40.8 jit_solution(15644519930898460395)
XLA Ops:
  0.0 39.1 %shard_map.46 = bf16[32,4,8,128]{3,2,1,0:T(8,128)(2,1)} custom-call(bf16[4,16,128]{2,1,0:T(8,128)(2,1)} %low_hbm.1, bf16[3456,128]{1,0:T(8,128)(2,1)} %w_hbm.1, bf16[128,384]{1,0:T(8,128)(2,1)} %ain_hbm.1, bf16[128,128]{1,0:T(8,128)(2,1)} %aout_hbm.1), custom_call_target="tpu_custom_call" | custom-call | tf_op jit(solution)/shard_map/pallas_call | solution.py:337
  39.1 1.7 %copy.5 = bf16[4,4,8,8,128]{4,3,2,1,0:T(8,128)(2,1)} copy(bf16[4,4,8,8,128]{4,3,1,2,0:T(8,128)(2,1)} %bitcast.4) | data formatting | bytes 524288 | tf_op jit(solution)/shard_map/transpose | solution.py:370
